TPU v7x, 128 devices: a whole 4x4x4 slice. The times are simulated.
128 devices in a mesh: row: 8 (over z, core), col: 16 (over x, y).
Axes of the slice: x: 4, y: 4, z: 4, core: 2. Of those that a mesh axis runs over, the one named last changes fastest.
Arguments:
- start_block: float32 [32768, 128], P(('row', 'col')), may hold values from -6 to 6
- degree: float32 [32768], P(('row', 'col')), may hold values from 3.99 to 4.01
- block_values: float32 [49152, 4096], P(('row', 'col')), may hold values from -0.0007324219 to 0.0007324219
- block_rows: int32 [49152], P(('row', 'col')), may hold values from 0 to 31
- block_slots: int32 [49152], P(('row', 'col')), may hold values from 0 to 31, as said below
- need_lists: int32 [2048, 2], P(('row', 'col')), may hold values from 0 to 4, as said below
- live_blocks: int32 [128], P(('row', 'col')), may hold values from 96 to 384, as said below
Outputs:
- alphas: float32 [2, 128, 128], replicated
- betas: float32 [2, 128, 128], replicated
- next_basis: float32 [32768, 128], P(('row', 'col'))
Inputs may be any that keep to these rules, and one draw needn't show every extreme that they name: `need_lists`: entries of a need list are distinct block rows, listed first, then padded with 4; every list has at least one entry, and on every device some list is full with 2 entries. `block_slots`: each slot's value p * 2 + q points at a listed (never padded) entry q of the device's need list p. `live_blocks`: some device uses all 384 slots in every draw.
All inputs are finite; a program needn't handle non-finite values.
Results may differ from a plain program's by a relative error of at most 0.00045.
Values sent between devices are 32-bit elements; how exact they have to be, the bound alone decides.
No kernel may reach another device: no remote copies, remote signals or barrier semaphores. Data moves between devices by JAX's collectives and lax.ppermute only.
A program may use at most 128 MiB of HBM per device.

v0:
```python
import jax
import jax.numpy as jnp
from jax import lax
from jax.sharding import PartitionSpec as P

BS = 64
ITERS = 2
HIGH = lax.Precision.HIGHEST


def local_gram(left, right):
    return jnp.einsum("ra,rb->ab", left, right, precision=HIGH)


def on_device(start_block, degree, block_values, block_rows, block_slots, need_lists, live_blocks):
    row_count = lax.axis_size("row")
    col_count = lax.axis_size("col")
    local_rows, block_width = start_block.shape
    owned_blocks = local_rows // BS
    list_length = need_lists.shape[1]
    capacity = block_values.shape[0]
    group_size = min(128, capacity)
    total_rows = local_rows * row_count * col_count
    live_count = live_blocks[0]
    flat_need = need_lists.reshape(-1)
    stripe_cols = block_slots // list_length * owned_blocks + flat_need[block_slots]
    start_gram = lax.psum(local_gram(start_block, start_block), ("row", "col")) / total_rows
    lower_factor = jnp.linalg.cholesky(start_gram)
    current = lax.linalg.triangular_solve(
        lower_factor, start_block, left_side=False, lower=True, transpose_a=True
    )
    basis_list = [current]
    alpha_list = []
    beta_list = []
    for iteration in range(ITERS):
        owned_rows = current.reshape(owned_blocks, BS, block_width)
        row_side = lax.all_gather(owned_rows, "row", axis=0, tiled=True)
        col_side = lax.all_gather(owned_rows, "col", axis=0, tiled=True)
        col_length = col_count * owned_blocks
        group_total = (live_count + group_size - 1) // group_size

        def group_step(group_index, partials):
            row_part, col_part = partials
            first_slot = group_index * group_size
            values_now = lax.dynamic_slice_in_dim(block_values, first_slot, group_size, 0).reshape(
                group_size, BS, BS
            )
            rows_now = lax.dynamic_slice_in_dim(block_rows, first_slot, group_size, 0)
            cols_now = lax.dynamic_slice_in_dim(stripe_cols, first_slot, group_size, 0)
            in_use = (first_slot + jnp.arange(group_size, dtype=jnp.int32) < live_count).astype(
                current.dtype
            )
            values_now = values_now * in_use[:, None, None]
            forward = jnp.einsum("sab,sbn->san", values_now, col_side[cols_now], precision=HIGH)
            backward = jnp.einsum("sba,sbn->san", values_now, row_side[rows_now], precision=HIGH)
            return (row_part.at[rows_now].add(forward), col_part.at[cols_now].add(backward))

        start_parts = (
            jnp.zeros((row_count * owned_blocks, BS, block_width), current.dtype),
            jnp.zeros((col_length, BS, block_width), current.dtype),
        )
        row_part, col_part = lax.fori_loop(0, group_total, group_step, start_parts)
        row_sum = lax.psum_scatter(row_part, "row", scatter_dimension=0, tiled=True)
        col_sum = lax.psum_scatter(col_part, "col", scatter_dimension=0, tiled=True)
        image_block = degree[:, None] * current - (row_sum + col_sum).reshape(
            local_rows, block_width
        )
        stacked = jnp.concatenate(basis_list, axis=1)
        alpha_block = lax.psum(local_gram(current, image_block), ("row", "col")) / total_rows
        image_block = image_block - jnp.dot(current, alpha_block, precision=HIGH)
        if iteration > 0:
            image_block = image_block - jnp.dot(basis_list[-2], beta_list[-1].T, precision=HIGH)
        projection = lax.psum(local_gram(stacked, image_block), ("row", "col")) / total_rows
        image_block = image_block - jnp.dot(stacked, projection, precision=HIGH)
        norm_gram = lax.psum(local_gram(image_block, image_block), ("row", "col")) / total_rows
        lower_factor = jnp.linalg.cholesky(norm_gram)
        current = lax.linalg.triangular_solve(
            lower_factor, image_block, left_side=False, lower=True, transpose_a=True
        )
        alpha_list.append(alpha_block)
        beta_list.append(lower_factor.T)
        basis_list.append(current)
    return (jnp.stack(alpha_list), jnp.stack(beta_list), current)


def solution(mesh):
    return jax.shard_map(
        on_device,
        mesh=mesh,
        in_specs=(
            P(("row", "col"), None),
            P(("row", "col")),
            P(("row", "col"), None),
            P(("row", "col")),
            P(("row", "col")),
            P(("row", "col"), None),
            P(("row", "col")),
        ),
        out_specs=(P(), P(), P(("row", "col"), None)),
        check_vma=False,
    )
```

profile of v0, /device:TPU:1, one launch (start us, length us, event | category | flops | bytes accessed | tf_op | source)
XLA Modules:
  0.0 1838.1 jit_solution(1668707022313247895)
XLA Ops:
  9.2 145.2 %all-reduce.8.cloned.1.call-done = f32[128,128]{0,1:T(8,128)} async-done(((f32[128,128]{0,1:T(8,128)}), f32[128,128]{0,1:T(8,128)}) %all-reduce.8.cloned.1.call-update) | async-done | bytes 65552 | tf_op jit(solution)/shard_map/psum | solution.py:27
  156.2 11.7 cholesky.59
  169.2 9.8 custom-call.7
  181.6 6.6 copy.70
  189.9 20.1 %fusion.27 = s32[384]{0:T(512)S(1)} fusion(s32[384]{0:T(512)S(1)} %copy-done.16, s32[]{:T(128)} %bitcast.7, s32[]{:T(128)} %bitcast.8, s32[]{:T(128)} %bitcast.9, s32[]{:T(128)} %bitcast.10, s32[]{:T(128)} %bitcast.11, s32[]{:T(128)} %bitcast.12, s32[]{:T(128)} %bitcast.13, s32[]{:T(128)} %bitcast.14, s32[]{:T(128)} %bitcast.15, s32[]{:T(128)} %bitcast.16, ...), kind=kLoop, calls=%fused_computation.85 | loop fusion | flops 31104 | bytes 3200 | tf_op jit(solution)/shard_map/add | solution.py:26
  210.0 37.6 %all-gather.5.cloned.1.call-done = f32[64,64,128]{2,1,0:T(8,128)} async-done(((f32[4,64,128]{2,1,0:T(8,128)}), f32[64,64,128]{2,1,0:T(8,128)}) %all-gather.5.cloned.1.call-update) | async-done | bytes 2097168 | tf_op jit(solution)/shard_map/all_gather | solution.py:38
  247.7 1.6 broadcast.95.clone
  249.3 130.8 %while.24 = (s32[]{:T(128)}, f32[32,64,128]{2,1,0:T(8,128)S(1)}, f32[64,64,128]{2,1,0:T(8,128)}, s32[]{:T(128)}, s32[384]{0:T(512)S(1)}, /*index=5*/f32[384,4096...) while((s32[]{:T(128)}, f32[32,64,128]{2,1,0:T(8,128)S(1)}, ...), condition=%wide.region_6.9_spmd, body=%wide.region_3.0_spmd.sunk | while | flops 1613237376 | bytes 96483616 | solution.py:62
  249.5 1.7 constant_dynamic-slice_fusion.4
  252.2 4.6 copy.103
  256.8 4.5 gather_fusion
  261.2 12.2 fusion.90
  273.4 13.5 scatter_fusion
  286.9 2.8 gather_fusion.1
  289.7 10.0 fusion.91
  299.8 13.5 scatter_fusion.1
  313.3 1.3 copy-done.9
  314.7 1.7 constant_dynamic-slice_fusion.4
  317.3 4.6 copy.103
  321.9 4.5 gather_fusion
  326.4 12.2 fusion.90
  338.5 13.5 scatter_fusion
  352.1 2.8 gather_fusion.1
  354.9 10.0 fusion.91
  364.9 13.5 scatter_fusion.1
  378.4 1.3 copy-done.9
  381.8 94.0 %reduce-scatter.5.cloned.1.call-done = f32[4,64,128]{2,1,0:T(8,128)} async-done(((f32[32,64,128]{2,1,0:T(8,128)}), f32[4,64,128]{2,1,0:T(8,128)}) %reduce-scatter.5.cloned.1.call-update) | async-done | bytes 131088 | tf_op jit(solution)/shard_map/reduce_scatter | solution.py:63
  475.7 77.8 %reduce-scatter.7.cloned.1.call-done = f32[4,64,128]{2,1,0:T(8,128)} async-done(((f32[64,64,128]{2,1,0:T(8,128)}), f32[4,64,128]{2,1,0:T(8,128)}) %reduce-scatter.7.cloned.1.call-update) | async-done | bytes 131088 | tf_op jit(solution)/shard_map/reduce_scatter | solution.py:64
  555.6 141.9 %all-reduce.10.cloned.1.call-done = f32[128,128]{0,1:T(8,128)} async-done(((f32[128,128]{0,1:T(8,128)}), f32[128,128]{0,1:T(8,128)}) %all-reduce.10.cloned.1.call-update) | async-done | bytes 65552 | tf_op jit(solution)/shard_map/psum | solution.py:69
  699.6 138.6 %all-reduce.12.cloned.1.call-done = f32[128,128]{0,1:T(8,128)} async-done(((f32[128,128]{0,1:T(8,128)}), f32[128,128]{0,1:T(8,128)}) %all-reduce.12.cloned.1.call-update) | async-done | bytes 65552 | tf_op jit(solution)/shard_map/psum | solution.py:73
  840.4 137.9 %all-reduce.14.cloned.1.call-done = f32[128,128]{0,1:T(8,128)} async-done(((f32[128,128]{0,1:T(8,128)}), f32[128,128]{0,1:T(8,128)}) %all-reduce.14.cloned.1.call-update) | async-done | bytes 65552 | tf_op jit(solution)/shard_map/psum | solution.py:75
  980.0 11.7 cholesky.70
  992.4 1.2 fusion.18
  993.6 9.8 custom-call.8
  1005.1 20.4 %all-gather.11.cloned.1.call-done = f32[32,64,128]{2,1,0:T(8,128)} async-done(((f32[4,64,128]{2,1,0:T(8,128)}), f32[32,64,128]{2,1,0:T(8,128)}) %all-gather.11.cloned.1.call-update) | async-done | bytes 1048592 | tf_op jit(solution)/shard_map/all_gather | solution.py:37
  1025.5 46.2 %all-gather.9.cloned.1.call-done = f32[64,64,128]{2,1,0:T(8,128)} async-done(((f32[4,64,128]{2,1,0:T(8,128)}), f32[64,64,128]{2,1,0:T(8,128)}) %all-gather.9.cloned.1.call-update) | async-done | bytes 2097168 | tf_op jit(solution)/shard_map/all_gather | solution.py:38
  1071.9 1.6 broadcast.95
  1073.5 130.6 %while.25 = (s32[]{:T(128)}, f32[32,64,128]{2,1,0:T(8,128)S(1)}, f32[64,64,128]{2,1,0:T(8,128)}, s32[]{:T(128)}, s32[384]{0:T(512)S(1)}, /*index=5*/f32[384,4096...) while((s32[]{:T(128)}, f32[32,64,128]{2,1,0:T(8,128)S(1)}, ...), condition=%wide.region_15.18_spmd, body=%wide.region_12.0_spmd.sunk | while | flops 1613237376 | bytes 96483616 | solution.py:62
  1073.7 1.7 constant_dynamic-slice_fusion.5
  1076.4 4.6 copy.104
  1080.9 4.5 gather_fusion.2
  1085.4 12.2 fusion.96
  1097.6 13.5 scatter_fusion.2
  1111.1 2.8 gather_fusion.3
  1113.9 10.0 fusion.97
  1123.9 13.5 scatter_fusion.3
  1137.5 1.3 copy-done.7
  1138.9 1.7 constant_dynamic-slice_fusion.5
  1141.5 4.6 copy.104
  1146.1 4.5 gather_fusion.2
  1150.5 12.2 fusion.96
  1162.7 13.5 scatter_fusion.2
  1176.2 2.8 gather_fusion.3
  1179.0 10.0 fusion.97
  1189.1 13.5 scatter_fusion.3
  1202.6 1.3 copy-done.7
  1205.7 94.0 %reduce-scatter.9.cloned.1.call-done = f32[4,64,128]{2,1,0:T(8,128)} async-done(((f32[32,64,128]{2,1,0:T(8,128)}), f32[4,64,128]{2,1,0:T(8,128)}) %reduce-scatter.9.cloned.1.call-update) | async-done | bytes 131088 | tf_op jit(solution)/shard_map/reduce_scatter | solution.py:63
  1299.7 77.7 %reduce-scatter.11.cloned.1.call-done = f32[4,64,128]{2,1,0:T(8,128)} async-done(((f32[64,64,128]{2,1,0:T(8,128)}), f32[4,64,128]{2,1,0:T(8,128)}) %reduce-scatter.11.cloned.1.call-update) | async-done | bytes 131088 | tf_op jit(solution)/shard_map/reduce_scatter | solution.py:64
  1379.5 142.1 %all-reduce.16.cloned.1.call-done = f32[128,128]{0,1:T(8,128)} async-done(((f32[128,128]{0,1:T(8,128)}), f32[128,128]{0,1:T(8,128)}) %all-reduce.16.cloned.1.call-update) | async-done | bytes 65552 | tf_op jit(solution)/shard_map/psum | solution.py:69
  1525.6 138.9 %all-reduce.18.cloned.1.call-done = f32[256,128]{1,0:T(8,128)} async-done(((f32[256,128]{1,0:T(8,128)}), f32[256,128]{1,0:T(8,128)}) %all-reduce.18.cloned.1.call-update) | async-done | bytes 131088 | tf_op jit(solution)/shard_map/psum | solution.py:73
  1664.4 1.3 convolution_subtract_fusion
  1667.5 137.4 %all-reduce.20.cloned.1.call-done = f32[128,128]{0,1:T(8,128)} async-done(((f32[128,128]{0,1:T(8,128)}), f32[128,128]{0,1:T(8,128)}) %all-reduce.20.cloned.1.call-update) | async-done | bytes 65552 | tf_op jit(solution)/shard_map/psum | solution.py:75
  1806.6 11.7 cholesky.81
  1820.5 9.8 custom-call.9
  (145 shorter events, 39.0 us)
Async XLA Ops:
  7.2 0.9 copy-start
  7.2 147.2 %all-reduce.8.cloned.1.call-start = ((), (), s32[]{:S(2)}) async-start(), calls=%async_computation.4 | async-start | bytes 131072 | tf_op jit(solution)/shard_map/psum | solution.py:27
  9.1 200.9 %all-gather.7.cloned.1.call-start = ((), (), s32[]{:S(2)}) async-start(), calls=%async_computation.6 | async-start | bytes 1179648 | tf_op jit(solution)/shard_map/all_gather | solution.py:37
  180.2 67.4 %all-gather.5.cloned.1.call-start = ((), (), s32[]{:S(2)}) async-start(), calls=%async_computation.5 | async-start | bytes 2228224 | tf_op jit(solution)/shard_map/all_gather | solution.py:38
  180.9 294.9 %reduce-scatter.5.cloned.1.call-start = ((), (), s32[]{:S(2)}) async-start(), calls=%async_computation.7 | async-start | bytes 1179648 | tf_op jit(solution)/shard_map/reduce_scatter | solution.py:63
  181.6 6.6 copy-start.17
  181.6 8.3 copy-start.16
  181.6 67.6 %copy-start.15 = (s32[384]{0:T(512)S(1)}, s32[384]{0:T(512)}, u32[]{:S(2)}) copy-start(s32[384]{0:T(512)} %param.17) | copy-start | bytes 4612
  249.3 305.3 %copy-start.14 = (f32[256]{0:T(256)S(1)}, f32[256]{0:T(256)}, u32[]{:S(2)}) copy-start(f32[256]{0:T(256)} %param.15) | copy-start | bytes 3076
  273.4 13.5 copy-start.4
  289.7 10.0 copy-start.8
  313.3 1.3 copy-start.9
  338.5 13.5 copy-start.4
  354.9 10.0 copy-start.8
  378.4 1.3 copy-start.9
  380.1 1.0 copy-start.3
  381.1 172.4 %reduce-scatter.7.cloned.1.call-start = ((), (), s32[]{:S(2)}) async-start(), calls=%async_computation.8 | async-start | bytes 2228224 | tf_op jit(solution)/shard_map/reduce_scatter | solution.py:64
  381.7 315.8 %all-reduce.10.cloned.1.call-start = ((), (), s32[]{:S(2)}) async-start(), calls=%async_computation.9 | async-start | bytes 131072 | tf_op jit(solution)/shard_map/psum | solution.py:69
  555.6 282.7 %all-reduce.12.cloned.1.call-start = ((), (), s32[]{:S(2)}) async-start(), calls=%async_computation.10 | async-start | bytes 131072 | tf_op jit(solution)/shard_map/psum | solution.py:73
  699.6 278.7 %all-reduce.14.cloned.1.call-start = ((), (), s32[]{:S(2)}) async-start(), calls=%async_computation.11 | async-start | bytes 131072 | tf_op jit(solution)/shard_map/psum | solution.py:75
  840.3 185.2 %all-gather.11.cloned.1.call-start = ((), (), s32[]{:S(2)}) async-start(), calls=%async_computation.13 | async-start | bytes 1179648 | tf_op jit(solution)/shard_map/all_gather | solution.py:37
  991.8 33.8 %copy-start.10 = (f32[128,128]{1,0:T(8,128)}, f32[128,128]{1,0:T(8,128)S(1)}, u32[]{:S(2)}) copy-start(f32[128,128]{1,0:T(8,128)S(1)} %cholesky.70) | copy-start | bytes 196612
  1004.5 67.3 %all-gather.9.cloned.1.call-start = ((), (), s32[]{:S(2)}) async-start(), calls=%async_computation.12 | async-start | bytes 2228224 | tf_op jit(solution)/shard_map/all_gather | solution.py:38
  1005.1 294.6 %reduce-scatter.9.cloned.1.call-start = ((), (), s32[]{:S(2)}) async-start(), calls=%async_computation.14 | async-start | bytes 1179648 | tf_op jit(solution)/shard_map/reduce_scatter | solution.py:63
  1097.6 13.5 copy-start.5
  1113.9 10.0 copy-start.6
  1137.5 1.3 copy-start.7
  1162.7 13.5 copy-start.5
  1179.0 10.0 copy-start.6
  1202.6 1.3 copy-start.7
  1204.1 1.0 copy-start.2
  1204.1 175.4 %copy-start.12 = (f32[128,128]{0,1:T(8,128)S(1)}, f32[128,128]{0,1:T(8,128)}, u32[]{:S(2)}) copy-start(f32[128,128]{0,1:T(8,128)} %all-reduce.10.cloned.1.call-done) | copy-start | bytes 196612
  1204.1 318.6 %copy-start.11 = (f32[128,128]{1,0:T(8,128)S(1)}, f32[128,128]{1,0:T(8,128)}, u32[]{:S(2)}) copy-start(f32[128,128]{1,0:T(8,128)} %copy-done.10) | copy-start | bytes 196612
  1204.1 615.6 %copy-start.13 = (f32[1,128,128]{1,2,0:T(8,128)S(1)}, f32[1,128,128]{1,2,0:T(8,128)}, u32[]{:S(2)}) copy-start(f32[1,128,128]{1,2,0:T(8,128)} %get-tuple-element.212) | copy-start | bytes 196612
  1205.1 172.3 %reduce-scatter.11.cloned.1.call-start = ((), (), s32[]{:S(2)}) async-start(), calls=%async_computation.15 | async-start | bytes 2228224 | tf_op jit(solution)/shard_map/reduce_scatter | solution.py:64
  1205.1 626.2 %copy-start.1 = (f32[256,128]{1,0:T(8,128)S(1)}, f32[256,128]{1,0:T(8,128)}, u32[]{:S(2)}) copy-start(f32[256,128]{1,0:T(8,128)} %param.14) | copy-start | bytes 393220
  1205.7 315.9 %all-reduce.16.cloned.1.call-start = ((), (), s32[]{:S(2)}) async-start(), calls=%async_computation.16 | async-start | bytes 131072 | tf_op jit(solution)/shard_map/psum | solution.py:69
  1379.5 285.0 %all-reduce.18.cloned.1.call-start = ((), (), s32[]{:S(2)}) async-start(), calls=%async_computation.17 | async-start | bytes 262144 | tf_op jit(solution)/shard_map/psum | solution.py:73
  1524.7 280.2 %all-reduce.20.cloned.1.call-start = ((), (), s32[]{:S(2)}) async-start(), calls=%async_computation.18 | async-start | bytes 131072 | tf_op jit(solution)/shard_map/psum | solution.py:75
Sparse Core Ops, SparseCore 0:
  13.3 141.0 all-reduce.7
  180.3 20.8 all-gather.6
  204.1 43.3 all-gather.4
  381.2 94.4 reduce-scatter.4
  479.2 74.2 reduce-scatter.6
  558.7 138.7 all-reduce.9
  703.6 134.6 all-reduce.11
  843.6 134.6 all-reduce.13
  1004.6 20.8 all-gather.10
  1028.3 43.4 all-gather.8
  1205.2 94.4 reduce-scatter.8
  1303.2 74.2 reduce-scatter.10
  1382.8 138.7 all-reduce.15
  1527.5 136.8 all-reduce.17
  1669.6 135.2 all-reduce.19
where the time goes:
time: 1850 us; the launch traced here: 1840 us
  waiting for transfers between devices  1430 us (77%)
  other arithmetic  209 us (11%)
  matrix products  102 us (6%)
  local copies, waits for them, and re-layouts  78.1 us (4%)
    psum x2, waiting for transfers between devices, on_device(): lax.psum(local_gram(current, image_block), ('row', 'col')) / total_rows  284 us
    psum x2, waiting for transfers between devices, on_device(): lax.psum(local_gram(stacked, image_block), ('row', 'col')) / total_rows  278 us
    psum x2, waiting for transfers between devices, on_device(): lax.psum(local_gram(image_block, image_block), ('row', 'col')) / total_rows  275 us
    reduce_scatter x2, waiting for transfers between devices, on_device(): row_sum = lax.psum_scatter(row_part, 'row', scatter_dimension=0, tiled=True)  188 us
    reduce_scatter x2, waiting for transfers between devices, on_device(): col_sum = lax.psum_scatter(col_part, 'col', scatter_dimension=0, tiled=True)  155 us
    psum x1, waiting for transfers between devices, on_device(): lax.psum(local_gram(start_block, start_block), ('row', 'col')) / total_rows  145 us
    all_gather x2, waiting for transfers between devices, on_device(): col_side = lax.all_gather(owned_rows, 'col', axis=0, tiled=True)  83.8 us
    scatter-add x4, other arithmetic, group_step(): col_part.at[cols_now].add(backward)  54 us
  transfers between devices with their start and end apart: 15, of which 14 were waited for; matrix products, arithmetic and copies ran while one was open for 2% of the time, Pallas kernels for 0%

commit v1 on v0

--- a/solution.py
+++ b/solution.py
@@ -24,7 +24,10 @@
     live_count = live_blocks[0]
     flat_need = need_lists.reshape(-1)
     stripe_cols = block_slots // list_length * owned_blocks + flat_need[block_slots]
-    start_gram = lax.psum(local_gram(start_block, start_block), ("row", "col")) / total_rows
+    start_gram = (
+        jnp.sum(lax.all_gather(local_gram(start_block, start_block), ("row", "col")), axis=0)
+        / total_rows
+    )
     lower_factor = jnp.linalg.cholesky(start_gram)
     current = lax.linalg.triangular_solve(
         lower_factor, start_block, left_side=False, lower=True, transpose_a=True

time: 1850 us -> 1780 us (0.962)
  waiting for transfers between devices: 1430 us -> 1360 us
    psum x1 -> x0, waiting for transfers between devices: 145 us -> none  [on_device(): lax.psum(local_gram(start_block, start_block), ('row', 'col')) / total_rows]
    all_gather x0 -> x1, waiting for transfers between devices: none -> 76.4 us  [on_device(): lax.all_gather(local_gram(start_block, start_block), ('row', 'col'))]
where the time goes in v1:
time: 1780 us; the launch traced here: 1770 us
  waiting for transfers between devices  1360 us (76%)
  other arithmetic  211 us (12%)
  matrix products  102 us (6%)
  local copies, waits for them, and re-layouts  78.2 us (4%)
    psum x2, waiting for transfers between devices, on_device(): lax.psum(local_gram(current, image_block), ('row', 'col')) / total_rows  286 us
    psum x2, waiting for transfers between devices, on_device(): lax.psum(local_gram(image_block, image_block), ('row', 'col')) / total_rows  277 us
    psum x2, waiting for transfers between devices, on_device(): lax.psum(local_gram(stacked, image_block), ('row', 'col')) / total_rows  276 us
    reduce_scatter x2, waiting for transfers between devices, on_device(): row_sum = lax.psum_scatter(row_part, 'row', scatter_dimension=0, tiled=True)  188 us
    reduce_scatter x2, waiting for transfers between devices, on_device(): col_sum = lax.psum_scatter(col_part, 'col', scatter_dimension=0, tiled=True)  155 us
    all_gather x2, waiting for transfers between devices, on_device(): col_side = lax.all_gather(owned_rows, 'col', axis=0, tiled=True)  83.6 us
    all_gather x1, waiting for transfers between devices, on_device(): lax.all_gather(local_gram(start_block, start_block), ('row', 'col'))  76.4 us
    scatter-add x4, other arithmetic, group_step(): col_part.at[cols_now].add(backward)  54 us
  transfers between devices with their start and end apart: 15, of which 14 were waited for; matrix products, arithmetic and copies ran while one was open for 2% of the time, Pallas kernels for 0%

profile of v1, /device:TPU:1, one launch (start us, length us, event | category | flops | bytes accessed | tf_op | source)
XLA Modules:
  0.0 1772.2 jit_solution(3497929272974036130)
XLA Ops:
  9.2 76.4 %all-gather.15.cloned.1.call-done = f32[16384,128]{1,0:T(8,128)} async-done(((f32[128,128]{1,0:T(8,128)}), f32[16384,128]{1,0:T(8,128)}) %all-gather.15.cloned.1.call-update) | async-done | bytes 8388624 | tf_op jit(solution)/shard_map/all_gather | solution.py:28
  85.5 3.8 reduce_sum.9
  89.6 11.7 cholesky.59
  102.6 9.8 custom-call.7
  115.0 6.6 copy.68
  123.3 20.1 %fusion.27 = s32[384]{0:T(512)S(1)} fusion(s32[384]{0:T(512)S(1)} %copy-done.16, s32[]{:T(128)} %bitcast.8, s32[]{:T(128)} %bitcast.9, s32[]{:T(128)} %bitcast.10, s32[]{:T(128)} %bitcast.11, s32[]{:T(128)} %bitcast.12, s32[]{:T(128)} %bitcast.13, s32[]{:T(128)} %bitcast.14, s32[]{:T(128)} %bitcast.15, s32[]{:T(128)} %bitcast.16, s32[]{:T(128)} %bitcast.17, ...), kind=kLoop, calls=%fused_computation.85 | loop fusion | flops 31104 | bytes 3200 | tf_op jit(solution)/shard_map/add | solution.py:26
  143.4 37.6 %all-gather.7.cloned.1.call-done = f32[64,64,128]{2,1,0:T(8,128)} async-done(((f32[4,64,128]{2,1,0:T(8,128)}), f32[64,64,128]{2,1,0:T(8,128)}) %all-gather.7.cloned.1.call-update) | async-done | bytes 2097168 | tf_op jit(solution)/shard_map/all_gather | solution.py:41
  181.0 1.6 broadcast.95.clone
  182.6 130.8 %while.24 = (s32[]{:T(128)}, f32[32,64,128]{2,1,0:T(8,128)S(1)}, f32[64,64,128]{2,1,0:T(8,128)}, s32[]{:T(128)}, s32[384]{0:T(512)S(1)}, /*index=5*/f32[384,4096...) while((s32[]{:T(128)}, f32[32,64,128]{2,1,0:T(8,128)S(1)}, ...), condition=%wide.region_6.9_spmd, body=%wide.region_3.0_spmd.sunk | while | flops 1613237376 | bytes 96483616 | solution.py:65
  182.9 1.7 constant_dynamic-slice_fusion.4
  185.6 4.6 copy.100
  190.1 4.5 gather_fusion
  194.6 12.2 fusion.90
  206.8 13.5 scatter_fusion
  220.3 2.8 gather_fusion.1
  223.1 10.0 fusion.91
  233.1 13.5 scatter_fusion.1
  246.6 1.3 copy-done.9
  248.0 1.7 constant_dynamic-slice_fusion.4
  250.7 4.6 copy.100
  255.3 4.5 gather_fusion
  259.7 12.2 fusion.90
  271.9 13.5 scatter_fusion
  285.4 2.8 gather_fusion.1
  288.2 10.0 fusion.91
  298.3 13.5 scatter_fusion.1
  311.8 1.3 copy-done.9
  315.1 94.0 %reduce-scatter.5.cloned.1.call-done = f32[4,64,128]{2,1,0:T(8,128)} async-done(((f32[32,64,128]{2,1,0:T(8,128)}), f32[4,64,128]{2,1,0:T(8,128)}) %reduce-scatter.5.cloned.1.call-update) | async-done | bytes 131088 | tf_op jit(solution)/shard_map/reduce_scatter | solution.py:66
  409.1 77.5 %reduce-scatter.7.cloned.1.call-done = f32[4,64,128]{2,1,0:T(8,128)} async-done(((f32[64,64,128]{2,1,0:T(8,128)}), f32[4,64,128]{2,1,0:T(8,128)}) %reduce-scatter.7.cloned.1.call-update) | async-done | bytes 131088 | tf_op jit(solution)/shard_map/reduce_scatter | solution.py:67
  488.6 142.7 %all-reduce.7.cloned.1.call-done = f32[128,128]{0,1:T(8,128)} async-done(((f32[128,128]{0,1:T(8,128)}), f32[128,128]{0,1:T(8,128)}) %all-reduce.7.cloned.1.call-update) | async-done | bytes 65552 | tf_op jit(solution)/shard_map/psum | solution.py:72
  633.4 137.9 %all-reduce.9.cloned.1.call-done = f32[128,128]{0,1:T(8,128)} async-done(((f32[128,128]{0,1:T(8,128)}), f32[128,128]{0,1:T(8,128)}) %all-reduce.9.cloned.1.call-update) | async-done | bytes 65552 | tf_op jit(solution)/shard_map/psum | solution.py:76
  773.4 138.6 %all-reduce.11.cloned.1.call-done = f32[128,128]{0,1:T(8,128)} async-done(((f32[128,128]{0,1:T(8,128)}), f32[128,128]{0,1:T(8,128)}) %all-reduce.11.cloned.1.call-update) | async-done | bytes 65552 | tf_op jit(solution)/shard_map/psum | solution.py:78
  913.8 11.7 cholesky.70
  927.4 9.8 custom-call.8
  938.9 20.4 %all-gather.13.cloned.1.call-done = f32[32,64,128]{2,1,0:T(8,128)} async-done(((f32[4,64,128]{2,1,0:T(8,128)}), f32[32,64,128]{2,1,0:T(8,128)}) %all-gather.13.cloned.1.call-update) | async-done | bytes 1048592 | tf_op jit(solution)/shard_map/all_gather | solution.py:40
  959.3 46.0 %all-gather.11.cloned.1.call-done = f32[64,64,128]{2,1,0:T(8,128)} async-done(((f32[4,64,128]{2,1,0:T(8,128)}), f32[64,64,128]{2,1,0:T(8,128)}) %all-gather.11.cloned.1.call-update) | async-done | bytes 2097168 | tf_op jit(solution)/shard_map/all_gather | solution.py:41
  1005.5 1.6 broadcast.95
  1007.0 130.6 %while.25 = (s32[]{:T(128)}, f32[32,64,128]{2,1,0:T(8,128)S(1)}, f32[64,64,128]{2,1,0:T(8,128)}, s32[]{:T(128)}, s32[384]{0:T(512)S(1)}, /*index=5*/f32[384,4096...) while((s32[]{:T(128)}, f32[32,64,128]{2,1,0:T(8,128)S(1)}, ...), condition=%wide.region_15.18_spmd, body=%wide.region_12.0_spmd.sunk | while | flops 1613237376 | bytes 96483616 | solution.py:65
  1007.3 1.7 constant_dynamic-slice_fusion.5
  1009.9 4.6 copy.101
  1014.5 4.5 gather_fusion.2
  1019.0 12.2 fusion.96
  1031.1 13.5 scatter_fusion.2
  1044.7 2.8 gather_fusion.3
  1047.5 10.0 fusion.97
  1057.5 13.5 scatter_fusion.3
  1071.0 1.3 copy-done.7
  1072.4 1.7 constant_dynamic-slice_fusion.5
  1075.1 4.6 copy.101
  1079.7 4.5 gather_fusion.2
  1084.1 12.2 fusion.96
  1096.3 13.5 scatter_fusion.2
  1109.8 2.8 gather_fusion.3
  1112.6 10.0 fusion.97
  1122.7 13.5 scatter_fusion.3
  1136.2 1.3 copy-done.7
  1139.3 94.0 %reduce-scatter.9.cloned.1.call-done = f32[4,64,128]{2,1,0:T(8,128)} async-done(((f32[32,64,128]{2,1,0:T(8,128)}), f32[4,64,128]{2,1,0:T(8,128)}) %reduce-scatter.9.cloned.1.call-update) | async-done | bytes 131088 | tf_op jit(solution)/shard_map/reduce_scatter | solution.py:66
  1233.3 77.5 %reduce-scatter.11.cloned.1.call-done = f32[4,64,128]{2,1,0:T(8,128)} async-done(((f32[64,64,128]{2,1,0:T(8,128)}), f32[4,64,128]{2,1,0:T(8,128)}) %reduce-scatter.11.cloned.1.call-update) | async-done | bytes 131088 | tf_op jit(solution)/shard_map/reduce_scatter | solution.py:67
  1312.8 142.8 %all-reduce.13.cloned.1.call-done = f32[128,128]{0,1:T(8,128)} async-done(((f32[128,128]{0,1:T(8,128)}), f32[128,128]{0,1:T(8,128)}) %all-reduce.13.cloned.1.call-update) | async-done | bytes 65552 | tf_op jit(solution)/shard_map/psum | solution.py:72
  1459.6 138.2 %all-reduce.15.cloned.1.call-done = f32[256,128]{1,0:T(8,128)} async-done(((f32[256,128]{1,0:T(8,128)}), f32[256,128]{1,0:T(8,128)}) %all-reduce.15.cloned.1.call-update) | async-done | bytes 131088 | tf_op jit(solution)/shard_map/psum | solution.py:76
  1597.8 1.3 convolution_subtract_fusion
  1600.8 138.1 %all-reduce.17.cloned.1.call-done = f32[128,128]{0,1:T(8,128)} async-done(((f32[128,128]{0,1:T(8,128)}), f32[128,128]{0,1:T(8,128)}) %all-reduce.17.cloned.1.call-update) | async-done | bytes 65552 | tf_op jit(solution)/shard_map/psum | solution.py:78
  1740.7 11.7 cholesky.81
  1754.6 9.8 custom-call.9
  (147 shorter events, 38.6 us)
Async XLA Ops:
  7.2 0.9 copy-start
  7.2 78.4 %all-gather.15.cloned.1.call-start = ((), (), s32[]{:S(2)}) async-start(), calls=%async_computation.18 | async-start | bytes 8454144 | tf_op jit(solution)/shard_map/all_gather | solution.py:28
  9.1 134.2 %all-gather.9.cloned.1.call-start = ((), (), s32[]{:S(2)}) async-start(), calls=%async_computation.5 | async-start | bytes 1179648 | tf_op jit(solution)/shard_map/all_gather | solution.py:40
  113.5 67.4 %all-gather.7.cloned.1.call-start = ((), (), s32[]{:S(2)}) async-start(), calls=%async_computation.4 | async-start | bytes 2228224 | tf_op jit(solution)/shard_map/all_gather | solution.py:41
  114.3 294.8 %reduce-scatter.5.cloned.1.call-start = ((), (), s32[]{:S(2)}) async-start(), calls=%async_computation.6 | async-start | bytes 1179648 | tf_op jit(solution)/shard_map/reduce_scatter | solution.py:66
  115.0 6.6 copy-start.17
  115.0 8.3 copy-start.16
  115.0 67.6 %copy-start.15 = (s32[384]{0:T(512)S(1)}, s32[384]{0:T(512)}, u32[]{:S(2)}) copy-start(s32[384]{0:T(512)} %param.17) | copy-start | bytes 4612
  182.6 305.0 %copy-start.14 = (f32[256]{0:T(256)S(1)}, f32[256]{0:T(256)}, u32[]{:S(2)}) copy-start(f32[256]{0:T(256)} %param.15) | copy-start | bytes 3076
  206.8 13.5 copy-start.4
  223.1 10.0 copy-start.8
  246.6 1.3 copy-start.9
  271.9 13.5 copy-start.4
  288.2 10.0 copy-start.8
  311.8 1.3 copy-start.9
  313.5 1.0 copy-start.3
  314.5 172.1 %reduce-scatter.7.cloned.1.call-start = ((), (), s32[]{:S(2)}) async-start(), calls=%async_computation.7 | async-start | bytes 2228224 | tf_op jit(solution)/shard_map/reduce_scatter | solution.py:67
  315.1 316.2 %all-reduce.7.cloned.1.call-start = ((), (), s32[]{:S(2)}) async-start(), calls=%async_computation.8 | async-start | bytes 131072 | tf_op jit(solution)/shard_map/psum | solution.py:72
  488.6 282.7 %all-reduce.9.cloned.1.call-start = ((), (), s32[]{:S(2)}) async-start(), calls=%async_computation.9 | async-start | bytes 131072 | tf_op jit(solution)/shard_map/psum | solution.py:76
  633.4 278.7 %all-reduce.11.cloned.1.call-start = ((), (), s32[]{:S(2)}) async-start(), calls=%async_computation.10 | async-start | bytes 131072 | tf_op jit(solution)/shard_map/psum | solution.py:78
  773.4 186.0 %all-gather.13.cloned.1.call-start = ((), (), s32[]{:S(2)}) async-start(), calls=%async_computation.12 | async-start | bytes 1179648 | tf_op jit(solution)/shard_map/all_gather | solution.py:40
  925.6 33.8 %copy-start.10 = (f32[128,128]{1,0:T(8,128)}, f32[128,128]{1,0:T(8,128)S(1)}, u32[]{:S(2)}) copy-start(f32[128,128]{1,0:T(8,128)S(1)} %cholesky.70) | copy-start | bytes 196612
  938.3 67.0 %all-gather.11.cloned.1.call-start = ((), (), s32[]{:S(2)}) async-start(), calls=%async_computation.11 | async-start | bytes 2228224 | tf_op jit(solution)/shard_map/all_gather | solution.py:41
  938.9 294.4 %reduce-scatter.9.cloned.1.call-start = ((), (), s32[]{:S(2)}) async-start(), calls=%async_computation.13 | async-start | bytes 1179648 | tf_op jit(solution)/shard_map/reduce_scatter | solution.py:66
  1031.1 13.5 copy-start.5
  1047.5 10.0 copy-start.6
  1071.0 1.3 copy-start.7
  1096.3 13.5 copy-start.5
  1112.6 10.0 copy-start.6
  1136.2 1.3 copy-start.7
  1137.7 1.0 copy-start.2
  1137.7 175.1 %copy-start.12 = (f32[128,128]{0,1:T(8,128)S(1)}, f32[128,128]{0,1:T(8,128)}, u32[]{:S(2)}) copy-start(f32[128,128]{0,1:T(8,128)} %all-reduce.7.cloned.1.call-done) | copy-start | bytes 196612
  1137.7 319.1 %copy-start.11 = (f32[128,128]{1,0:T(8,128)S(1)}, f32[128,128]{1,0:T(8,128)}, u32[]{:S(2)}) copy-start(f32[128,128]{1,0:T(8,128)} %copy-done.10) | copy-start | bytes 196612
  1137.7 616.1 %copy-start.13 = (f32[1,128,128]{1,2,0:T(8,128)S(1)}, f32[1,128,128]{1,2,0:T(8,128)}, u32[]{:S(2)}) copy-start(f32[1,128,128]{1,2,0:T(8,128)} %get-tuple-element.212) | copy-start | bytes 196612
  1138.7 172.1 %reduce-scatter.11.cloned.1.call-start = ((), (), s32[]{:S(2)}) async-start(), calls=%async_computation.14 | async-start | bytes 2228224 | tf_op jit(solution)/shard_map/reduce_scatter | solution.py:67
  1138.7 626.7 %copy-start.1 = (f32[256,128]{1,0:T(8,128)S(1)}, f32[256,128]{1,0:T(8,128)}, u32[]{:S(2)}) copy-start(f32[256,128]{1,0:T(8,128)} %param.14) | copy-start | bytes 393220
  1139.2 316.4 %all-reduce.13.cloned.1.call-start = ((), (), s32[]{:S(2)}) async-start(), calls=%async_computation.15 | async-start | bytes 131072 | tf_op jit(solution)/shard_map/psum | solution.py:72
  1312.8 285.0 %all-reduce.15.cloned.1.call-start = ((), (), s32[]{:S(2)}) async-start(), calls=%async_computation.16 | async-start | bytes 262144 | tf_op jit(solution)/shard_map/psum | solution.py:76
  1458.7 280.2 %all-reduce.17.cloned.1.call-start = ((), (), s32[]{:S(2)}) async-start(), calls=%async_computation.17 | async-start | bytes 131072 | tf_op jit(solution)/shard_map/psum | solution.py:78
Sparse Core Ops, SparseCore 0:
  11.7 73.7 all-gather.14
  113.7 21.0 all-gather.8
  137.5 43.4 all-gather.6
  314.6 94.4 reduce-scatter.4
  412.2 74.3 reduce-scatter.6
  492.4 138.8 all-reduce.6
  636.6 134.6 all-reduce.8
  777.3 134.6 all-reduce.10
  938.4 20.8 all-gather.12
  961.9 43.4 all-gather.10
  1138.8 94.4 reduce-scatter.8
  1236.4 74.3 reduce-scatter.10
  1316.8 138.8 all-reduce.12
  1460.8 136.9 all-reduce.14
  1603.7 135.2 all-reduce.16
